TPU v7x, 256 devices: a whole 4x4x8 slice. The times are simulated.
256 devices in a mesh: row: 8 (over x, core), col: 32 (over y, z).
Axes of the slice: x: 4, y: 4, z: 8, core: 2. Of those that a mesh axis runs over, the one named last changes fastest.
Arguments:
- step: int32 [1], replicated, may hold values from 0 to 28
- rhs: float32 [12288, 27648], P('row', 'col'), may hold values from -6 to 6
- panels: float32 [12288, 8192], P('row', 'col'), may hold values from -0.375 to 0.375
- diag_inverses: float32 [256, 8192], P(None, 'col'), may hold values from -2 to 2, as said below
Outputs:
- updated: float32 [12288, 27648], P('row', 'col')
Inputs may be any that keep to these rules, and one draw needn't show every extreme that they name: `diag_inverses`: each 256-column block is lower triangular with a positive diagonal.
All inputs are finite; a program needn't handle non-finite values.
Results may differ from a plain program's by a relative error of at most 0.00018.
Values sent between devices are 32-bit elements; how exact they have to be, the bound alone decides.
A program may use at most 128 MiB of HBM per device.

v0:
```python
import jax
import jax.numpy as jnp
from jax import lax
from jax.sharding import PartitionSpec as P

STEPS = 4


def broadcast(value, axis, root):
    mine = lax.axis_index(axis) == root
    return lax.psum(jnp.where(mine, value, jnp.zeros_like(value)), axis)


def apply_column(column, operand):
    return jnp.einsum("bij,jk->bik", column, operand, precision=lax.Precision.HIGHEST)


def body(step, rhs, panels, diag_inverses):
    n_row = lax.axis_size("row")
    my_row = lax.axis_index("row")
    width = diag_inverses.shape[0]
    blk_local = rhs.shape[0] // width
    cols_local = rhs.shape[1]
    y_blocks = rhs.reshape(blk_local, width, cols_local)
    column_local = panels.reshape(blk_local, width, width)
    global_block = jnp.arange(blk_local, dtype=jnp.int32) * n_row + my_row
    start = step[0]
    for turn in range(STEPS):
        k = start + turn
        owner_row = k % n_row
        local_k = k // n_row
        block_k = lax.dynamic_index_in_dim(y_blocks, local_k, 0, keepdims=False)
        column, inverse = (broadcast(column_local, "col", k), broadcast(diag_inverses, "col", k))
        solved = jnp.dot(
            inverse, block_k, precision=lax.Precision.HIGHEST, preferred_element_type=jnp.float32
        )
        solved = broadcast(solved, "row", owner_row)
        change = apply_column(column, solved)
        y_blocks = jnp.where((global_block > k)[:, None, None], y_blocks - change, y_blocks)
        y_blocks = jnp.where((global_block == k)[:, None, None], solved[None], y_blocks)
    return y_blocks.reshape(blk_local * width, cols_local)


def solution(mesh):
    in_specs = (P(), P("row", "col"), P("row", "col"), P(None, "col"))
    out_specs = P("row", "col")
    return jax.shard_map(body, mesh=mesh, in_specs=in_specs, out_specs=out_specs, check_vma=False)
```

profile of v0, /device:TPU:8, one launch (start us, length us, event | category | flops | bytes accessed | tf_op | source)
XLA Modules:
  0.0 550.3 jit_solution(6518097314178921383)
XLA Ops:
  7.2 4.2 broadcast_select_fusion
  11.5 1.0 broadcast_select_fusion.7
  12.5 0.0 all-reduce.15.cloned.1.call-update
  12.5 0.0 all-reduce.7.cloned.1.call-start
  12.6 6.1 %copy.5 = f32[1536,864]{1,0:T(8,128)} copy(f32[1536,864]{0,1:T(8,128)} %param.5) | data formatting | bytes 10616832 | tf_op args[1]
  18.7 197.7 %all-reduce.15.cloned.1.call-done = (f32[256,256]{1,0:T(8,128)}, f32[6,256,256]{2,1,0:T(8,128)}, f32[256,256]{1,0:T(8,128)}, f32[6,256,256]{2,1,0:T(8,128)}, f32...) async-done(((f32[256,256]{1,0:T(8,128)}, f32[6,256,256]{2,1,0:T(8,128)}, f32[256,256]{1,0:T(8,128)}, ...) | async-done | bytes 7340048 | tf_op jit(solution)/shard_map/psum | solution.py:11
  216.3 3.9 convolution_select_fusion.3
  220.2 0.0 all-reduce.7.cloned.1.call-update
  220.2 0.0 all-reduce.9.cloned.1.call-start
  220.3 6.1 %copy.6 = f32[6,256,864]{1,2,0:T(8,128)} copy(f32[6,256,864]{2,1,0:T(8,128)} %bitcast.49) | data formatting | bytes 10616832 | tf_op jit(solution)/shard_map/reshape | solution.py:24
  226.4 59.8 %all-reduce.7.cloned.1.call-done = f32[256,864]{0,1:T(8,128)} async-done(((f32[256,864]{0,1:T(8,128)}), f32[256,864]{0,1:T(8,128)}) %all-reduce.7.cloned.1.call-update) | async-done | bytes 884752 | tf_op jit(solution)/shard_map/psum | solution.py:11
  286.3 8.3 %fusion = f32[6,256,864]{1,2,0:T(8,128)S(1)} fusion(f32[6,256,864]{1,2,0:T(8,128)} %copy.6, f32[256,864]{0,1:T(8,128)} %all-reduce.7.cloned.1.call-done, pred[6]{0:T(512)(128)(4,1)S(1)} %get-tuple-element.21, pred[6]{0:T(512)(128)(4,1)S(1)} %get-tuple-element.22, f32[6,256,256]{2,1,0:T(8,128)S(1)} %copy-done.6), kind=kOutput, calls=%fused_computation.4 | convolution fusion | flops 4080844800 | bytes 13074444 | tf_op jit(solution)/shard_map/bij,jk->bik/dot_general | solution.py:15
  294.6 0.0 copy-start.1
  294.6 2.4 copy-done.1
  297.0 1.9 convolution_select_fusion.2
  298.8 0.0 all-reduce.9.cloned.1.call-update
  298.9 0.0 all-reduce.11.cloned.1.call-start
  299.0 66.0 %all-reduce.9.cloned.1.call-done = f32[256,864]{0,1:T(8,128)} async-done(((f32[256,864]{0,1:T(8,128)}), f32[256,864]{0,1:T(8,128)}) %all-reduce.9.cloned.1.call-update) | async-done | bytes 884752 | tf_op jit(solution)/shard_map/psum | solution.py:11
  365.0 8.3 %fusion.1 = f32[6,256,864]{1,2,0:T(8,128)S(1)} fusion(f32[6,256,864]{1,2,0:T(8,128)} %copy-done.1, f32[256,864]{0,1:T(8,128)} %all-reduce.9.cloned.1.call-done, pred[6]{0:T(512)(128)(4,1)S(1)} %get-tuple-element.27, pred[6]{0:T(512)(128)(4,1)S(1)} %get-tuple-element.28, f32[6,256,256]{2,1,0:T(8,128)S(1)} %copy-done.5), kind=kOutput, calls=%fused_computation.5 | convolution fusion | flops 4080844800 | bytes 13074444 | tf_op jit(solution)/shard_map/bij,jk->bik/dot_general | solution.py:15
  373.3 2.4 copy-done
  375.7 1.9 convolution_select_fusion.1
  377.5 0.0 all-reduce.11.cloned.1.call-update
  377.6 0.2 all-reduce.13.cloned.1.call-start
  377.9 65.8 %all-reduce.11.cloned.1.call-done = f32[256,864]{0,1:T(8,128)} async-done(((f32[256,864]{0,1:T(8,128)}), f32[256,864]{0,1:T(8,128)}) %all-reduce.11.cloned.1.call-update) | async-done | bytes 884752 | tf_op jit(solution)/shard_map/psum | solution.py:11
  443.7 8.3 %fusion.2 = f32[6,256,864]{1,2,0:T(8,128)S(1)} fusion(f32[6,256,864]{1,2,0:T(8,128)} %copy-done, f32[256,864]{0,1:T(8,128)} %all-reduce.11.cloned.1.call-done, pred[6]{0:T(512)(128)(4,1)S(1)} %get-tuple-element.25, pred[6]{0:T(512)(128)(4,1)S(1)} %get-tuple-element.26, f32[6,256,256]{2,1,0:T(8,128)S(1)} %copy-done.4), kind=kOutput, calls=%fused_computation.6 | convolution fusion | flops 4080844800 | bytes 13074444 | tf_op jit(solution)/shard_map/bij,jk->bik/dot_general | solution.py:15
  452.0 2.4 copy-done.2
  454.4 1.9 convolution_select_fusion
  456.2 0.0 all-reduce.13.cloned.1.call-update
  456.3 66.1 %all-reduce.13.cloned.1.call-done = f32[256,864]{0,1:T(8,128)} async-done(((f32[256,864]{0,1:T(8,128)}), f32[256,864]{0,1:T(8,128)}) %all-reduce.13.cloned.1.call-update) | async-done | bytes 884752 | tf_op jit(solution)/shard_map/psum | solution.py:11
  522.4 9.4 %fusion.3 = f32[6,256,864]{1,2,0:T(8,128)} fusion(f32[6,256,864]{1,2,0:T(8,128)} %copy-done.2, f32[256,864]{0,1:T(8,128)} %all-reduce.13.cloned.1.call-done, pred[6]{0:T(512)(128)(4,1)S(1)} %get-tuple-element.23, pred[6]{0:T(512)(128)(4,1)S(1)} %get-tuple-element.24, f32[6,256,256]{2,1,0:T(8,128)S(1)} %copy-done.3), kind=kOutput, calls=%fused_computation.7 | convolution fusion | flops 4080844800 | bytes 13074444 | tf_op jit(solution)/shard_map/bij,jk->bik/dot_general | solution.py:15
  531.8 6.1 %copy.8 = f32[6,256,864]{2,1,0:T(8,128)} copy(f32[6,256,864]{1,2,0:T(8,128)} %fusion.3) | data formatting | bytes 10616832 | tf_op jit(solution)/shard_map/jit(_where)/select_n | solution.py:40
  537.8 6.0 %copy.9 = f32[1536,864]{0,1:T(8,128)} copy(f32[1536,864]{1,0:T(8,128)} %bitcast.50) | data formatting | bytes 10616832 | tf_op jit(solution)/shard_map/reshape | solution.py:41
  (23 shorter events, 0.1 us)
Async XLA Ops:
  6.5 4.9 copy-start.7
  6.5 209.8 %all-reduce.15.cloned.1.call-start = ((), (), s32[]{:S(2)}) async-start(), calls=%async_computation.4 | async-start | bytes 14680064 | tf_op jit(solution)/shard_map/psum | solution.py:11
  12.5 273.7 %all-reduce.7.cloned.1.call-start = ((), (), s32[]{:S(2)}) async-start(), calls=%async_computation | async-start | bytes 1769472 | tf_op jit(solution)/shard_map/psum | solution.py:11
  220.2 66.0 %copy-start.6 = (f32[6,256,256]{2,1,0:T(8,128)S(1)}, f32[6,256,256]{2,1,0:T(8,128)}, u32[]{:S(2)}) copy-start(f32[6,256,256]{2,1,0:T(8,128)} %get-tuple-element.6) | copy-start | bytes 4718596
  220.2 144.7 %all-reduce.9.cloned.1.call-start = ((), (), s32[]{:S(2)}) async-start(), calls=%async_computation.1 | async-start | bytes 1769472 | tf_op jit(solution)/shard_map/psum | solution.py:11
  286.3 10.7 %copy-start.10 = (f32[256,256]{1,0:T(8,128)S(1)}, f32[256,256]{1,0:T(8,128)}, u32[]{:S(2)}) copy-start(f32[256,256]{1,0:T(8,128)} %get-tuple-element.7) | copy-start | bytes 786436
  286.3 78.7 %copy-start.5 = (f32[6,256,256]{2,1,0:T(8,128)S(1)}, f32[6,256,256]{2,1,0:T(8,128)}, u32[]{:S(2)}) copy-start(f32[6,256,256]{2,1,0:T(8,128)} %get-tuple-element.8) | copy-start | bytes 4718596
  294.6 2.4 copy-start.1
  298.9 144.8 %all-reduce.11.cloned.1.call-start = ((), (), s32[]{:S(2)}) async-start(), calls=%async_computation.2 | async-start | bytes 1769472 | tf_op jit(solution)/shard_map/psum | solution.py:11
  365.0 10.7 %copy-start.9 = (f32[256,256]{1,0:T(8,128)S(1)}, f32[256,256]{1,0:T(8,128)}, u32[]{:S(2)}) copy-start(f32[256,256]{1,0:T(8,128)} %get-tuple-element.9) | copy-start | bytes 786436
  365.0 78.7 %copy-start.4 = (f32[6,256,256]{2,1,0:T(8,128)S(1)}, f32[6,256,256]{2,1,0:T(8,128)}, u32[]{:S(2)}) copy-start(f32[6,256,256]{2,1,0:T(8,128)} %get-tuple-element.10) | copy-start | bytes 4718596
  373.3 2.4 copy-start
  377.6 144.8 %all-reduce.13.cloned.1.call-start = ((), (), s32[]{:S(2)}) async-start(), calls=%async_computation.3 | async-start | bytes 1769472 | tf_op jit(solution)/shard_map/psum | solution.py:11
  443.7 10.7 %copy-start.8 = (f32[256,256]{1,0:T(8,128)S(1)}, f32[256,256]{1,0:T(8,128)}, u32[]{:S(2)}) copy-start(f32[256,256]{1,0:T(8,128)} %get-tuple-element.11) | copy-start | bytes 786436
  443.7 78.7 %copy-start.3 = (f32[6,256,256]{2,1,0:T(8,128)S(1)}, f32[6,256,256]{2,1,0:T(8,128)}, u32[]{:S(2)}) copy-start(f32[6,256,256]{2,1,0:T(8,128)} %get-tuple-element.12) | copy-start | bytes 4718596
  452.0 2.4 copy-start.2
Sparse Core Ops, SparseCore 0:
  12.6 203.6 all-reduce.14
  220.3 65.8 all-reduce.6
  299.0 65.9 all-reduce.8
  377.7 65.9 all-reduce.10
  456.4 65.9 all-reduce.12
where the time goes:
time: 551 us; the launch traced here: 550 us
  waiting for transfers between devices  455 us (83%)
  matrix products  43.8 us (8%)
  local copies, waits for them, and re-layouts  31.4 us (6%)
  between operations  14.1 us (3%)
    psum x5, waiting for transfers between devices, broadcast(): return lax.psum(jnp.where(mine, value, jnp.zeros_like(value)), axis)  455 us
    dot_general x4, matrix products, apply_column(): jnp.einsum('bij,jk->bik', column, operand, precision=lax.Precision.HIGHEST)  34.3 us
    unnamed x23, local copies, waits for them, and re-layouts  13.2 us
  transfers between devices with their start and end apart: 5, of which 5 were waited for; matrix products, arithmetic and copies ran while one was open for 2% of the time, Pallas kernels for 0%

commit v1 on v0

v1 whole, which is shorter than its diff:
```python
import functools

import jax
import jax.numpy as jnp
from jax import lax
from jax.experimental import pallas as pl
from jax.experimental.pallas import tpu as pltpu
from jax.sharding import PartitionSpec as P

STEPS = 4
NB = 256
BLK = 6
MESH = pl.DeviceIdType.MESH
SPLIT = 640
WIDE = 1024
REST = WIDE - SPLIT
SEGMENTS = [
    [(True, 0, 0, 256)],
    [(True, 256, 0, 256)],
    [(True, 512, 0, 128), (False, 0, 128, 128)],
    [(False, 128, 0, 256)],
]
PAIRS = [(1, 0), (2, 0), (2, 1), (3, 0), (3, 1), (3, 2)]


def device(x, core, y, z):
    return (lax.rem(x + 8, 4) * 2 + core, lax.rem(y + 8, 4) * 8 + lax.rem(z + 16, 8))


def halve(value):
    high = value.astype(jnp.bfloat16)
    return high, (value - high.astype(jnp.float32)).astype(jnp.bfloat16)


def product(a, b):
    dot = functools.partial(
        lax.dot_general, dimension_numbers=(((1,), (1,)), ((), ())), preferred_element_type=jnp.float32)
    return dot(a[0], b[0]) + (dot(a[0], b[1]) + dot(a[1], b[0]))


def choose(index, values):
    result = values[0]
    for n, value in enumerate(values[1:], 1):
        result = jnp.where(index == n, value, result)
    return result


def step_kernel(step, panels, diag, rhs, out, r0, r1, r2, s0, s1, s2, p0, p1, p2, a1, b1, a2, b2, gathered,
                tc, tall, ycand, ypart, yhalf, ysel, solved, high, low, f_high, f_low, acc, send, recv,
                local):
    start = step[0]
    row, col = lax.axis_index("row"), lax.axis_index("col")
    x, core = row // 2, lax.rem(row, 2)
    y, z = col // 8, lax.rem(col, 8)
    row_step = lax.rem(row - start + 32, 4)
    row_block = start + row_step
    row_local = row_block // 8
    row_real = lax.rem(row_block, 8) == row
    col_block = start + lax.rem(z - start + 32, 4)
    col_y = col_block // 8
    used = [0]
    sent = []

    def take(n=1):
        used[0] += n
        return used[0] - n

    def remote(src, dst, index, target):
        return pltpu.make_async_remote_copy(
            src_ref=src, dst_ref=dst, send_sem=send.at[index], recv_sem=recv.at[index],
            device_id=target, device_id_type=MESH)

    def push(src, dst, target):
        copy = remote(src, dst, take(), target)
        copy.start()
        sent.append(copy)
        return copy

    def arrived(copies):
        for copy in copies:
            copy.wait_recv()

    def at(dy=0, dz=0):
        return device(x, core, y + dy, z + dz)

    def across(dx=0, dc=0):
        return device(x + dx, lax.rem(core + dc, 2), y, z)

    barrier = pltpu.get_barrier_semaphore()
    others = [(dx, dc) for dx in range(4) for dc in (0, 1) if dx or dc]
    friends = [at(dy=d) for d in (1, -1, 2)] + [at(dz=d) for d in range(1, 8)] + [across(*o) for o in others]
    for friend in friends:
        pl.semaphore_signal(barrier, inc=1, device_id=friend, device_id_type=MESH)
    loads = [pltpu.make_async_copy(rhs.at[:, pl.ds(NB * l, NB)], acc.at[:, pl.ds(NB * l, NB)], local.at[l])
             for l in range(BLK)]
    for load in loads:
        load.start()
    tc[0] = diag[0]
    for ty in range(4):
        tc[1, ty] = choose(row_local, [panels[l, ty] for l in range(4)])
    pl.semaphore_wait(barrier, len(friends))

    class Scatter:
        def __init__(self, src, first, n, landing, stage, landed):
            self.src, self.first, self.n = src, first, n
            self.landing, self.stage, self.landed = landing, stage, landed

        def along_y(self):
            blocks = pl.ds(self.first, self.n)
            self.copies = [push(self.src.at[blocks, lax.rem(y + d + 4, 4)], self.landing.at[k], at(dy=d))
                           for k, d in enumerate((1, -1, 2))]

        def along_z(self):
            arrived(self.copies)
            back = lax.rem(y - col_y + 4, 4)
            for p in range(self.n):
                for tz in range(8):
                    self.stage[tz, p] = choose(back, [self.src[self.first + p, y, tz]] + [
                        self.landing[k, p, tz] for k in (0, 2, 1)])
            self.copies = [push(self.stage.at[lax.rem(z + d, 8)], self.landed.at[z], at(dz=d)) for d in range(1, 8)]
            self.landed[z] = self.stage[z]

        def arrive(self):
            arrived(self.copies)

        def pick(self, i, p):
            return choose(lax.rem(start + i, 8), [self.landed[n, p] for n in range(8)])

    class Chunk:
        def __init__(self, a, b, width, cut):
            self.a, self.b, self.width, self.cut = a, b, width, cut
            self.a_z, self.a_y, self.a_far, self.b_y, self.b_z = {}, {}, [], [], {}

        def move(self, ref, dy, dz):
            return push(ref, ref, at(dy=dy, dz=dz))

        def send_a_z(self, t):
            right, left = lax.rem(z - (t - 1) + 8, 8), lax.rem(z + (t - 1), 8)
            if t < 4:
                lanes = (pl.ds(0, self.width), pl.ds(0, self.width))
            else:
                lanes = (pl.ds(0, self.cut), pl.ds(self.cut, self.width - self.cut))
            self.a_z[t] = [self.move(self.a.at[y, right, :, :, lanes[0]], 0, 1),
                           self.move(self.a.at[y, left, :, :, lanes[1]], 0, -1)]

        def send_b_z(self, t):
            right, left = lax.rem(z - (t - 1) + 8, 8), lax.rem(z + (t - 1), 8)
            rows = (pl.ds(0, 4), pl.ds(0, 4)) if t < 4 else (pl.ds(0, 2), pl.ds(2, 2))
            self.b_z[t] = [self.move(self.b.at[right, rows[0]], 0, 1), self.move(self.b.at[left, rows[1]], 0, -1)]

        def send_a_y(self, t):
            origins = [lax.rem(z - t + 8, 8), lax.rem(z + t, 8)]
            if t in (0, 4):
                origins = origins[:1]
            self.a_y[t] = [self.move(self.a.at[y, o], d, 0) for o in origins for d in (1, -1)]

        def send_a_far(self, t):
            below, above = lax.rem(y + 3, 4), lax.rem(y + 1, 4)
            if t < 4:
                self.a_far.append(self.move(self.a.at[below, lax.rem(z - t + 8, 8)], 1, 0))
            if t > 0:
                self.a_far.append(self.move(self.a.at[above, lax.rem(z + t, 8)], -1, 0))

        def begin(self):
            self.send_a_z(1)
            if self.b is not None:
                self.b_y = [self.move(self.b.at[z, y], d, 0) for d in (1, -1, 2)]
            self.send_a_y(0)

        def step(self, t):
            if t <= 4:
                arrived(self.a_z[t])
                if t < 4:
                    self.send_a_z(t + 1)
                self.send_a_y(t)
            if self.b is not None:
                arrived(self.b_y if t == 1 else self.b_z[t - 1])
                if t <= 4:
                    self.send_b_z(t)
            arrived(self.a_y[t - 1])
            self.send_a_far(t - 1)

        def end(self):
            arrived(self.a_far)

    small = Scatter(tc, 0, 2, r0, s0, p0)
    first = Scatter(panels, 0, 3, r1, s1, p1)
    second = Scatter(panels, 3, 3, r2, s2, p2)
    g = Chunk(gathered.at[core], None, NB, 128)
    c1 = Chunk(a1, b1, SPLIT, 384)
    c2 = Chunk(a2, b2, SPLIT, 384)

    def place(scatter, a, b):
        for i in range(STEPS):
            for p in range(3):
                value = scatter.pick(i, p)
                for in_a, lane, source, n in SEGMENTS[i]:
                    part = value[:, source:source + n]
                    if in_a:
                        a[y, z, p, :, lane:lane + n] = part
                    else:
                        b[z, y, p, :, lane:lane + n] = part

    half = rhs.shape[0] // 2
    side = x // 2

    def candidates():
        for load in loads:
            load.wait()
        for h in (0, 1):
            ycand[h] = choose(row_local, [acc[pl.ds(half * h, half), pl.ds(NB * l, NB)] for l in range(4)])
        return push(ycand.at[1 - side], ypart, across(dx=2))

    def share(copy):
        arrived([copy])
        yhalf[...] = jnp.where(row_real, ycand[side], ypart[...])
        slot = lax.rem(row, 4)
        copies = [push(yhalf, ysel.at[slot, side], across(dx=d)) for d in (1, 3, 2)]
        copies.append(push(yhalf, ysel.at[slot, side], across(dc=1)))
        ysel[slot, side] = yhalf[...]
        return copies

    def relay(copies):
        arrived(copies[:3])
        passed = []
        for d in (1, 3, 2):
            sx = lax.rem(x - d + 4, 4)
            ref = ysel.at[lax.rem(2 * sx + core, 4), sx // 2]
            passed.append(push(ref, ref, across(dc=1)))
        return [copies[3]] + passed

    def triangle():
        for i in range(STEPS):
            tall[row, i] = small.pick(i, 1)
        return [push(tall.at[row], tall.at[row], across(*o)) for o in others]

    def payload():
        for m in range(2):
            gathered[core, y, z, m] = small.pick(2 * core + m, 0)
        for m in range(3):
            i = jnp.where(core == 0, PAIRS[m][0], PAIRS[3 + m][0])
            j = jnp.where(core == 0, PAIRS[m][1], PAIRS[3 + m][1])
            gathered[core, y, z, 2 + m] = choose(lax.rem(start + i, 8), [tall[n, j] for n in range(8)])

    def square(c, m):
        return halve(gathered[c, :, :, m].reshape(NB, NB))

    def solve(i):
        lanes = pl.ds(NB * i, NB)
        right = choose(lax.rem(start + i, 4), [ysel[n].reshape(2 * half, NB) for n in range(4)])
        for index, (k, j) in enumerate(PAIRS):
            if k == i:
                before = pl.ds(NB * j, NB)
                right = right - product((high[:, before], low[:, before]), square(index // 3, 2 + index % 3))
        value = product(halve(right), square(i // 2, i % 2))
        solved[...] = value if i == 0 else jnp.where(row_step == i, value, solved[...])
        high[:, lanes], low[:, lanes] = halve(value)

    def assemble(chunk, p, block):
        for ty in range(4):
            rows = pl.ds(64 * ty, 64)
            for i in range(STEPS):
                keep = start + i < block
                for in_a, lane, source, n in SEGMENTS[i]:
                    if in_a:
                        value = chunk.a[ty, :, p, :, lane:lane + n]
                    else:
                        value = chunk.b[:, ty, p, :, lane:lane + n]
                    value = jnp.where(keep, value.reshape(64, n), 0.0)
                    to = pl.ds(NB * i + source, n)
                    f_high[rows, to], f_low[rows, to] = halve(value)

    def store(l):
        return pltpu.make_async_copy(acc.at[:, pl.ds(NB * l, NB)], out.at[:, pl.ds(NB * l, NB)], local.at[8 + l])

    def update(chunk, p, l):
        assemble(chunk, p, l * 8 + row)
        lanes = pl.ds(NB * l, NB)
        value = acc[:, lanes] - product((high[...], low[...]), (f_high[...], f_low[...]))
        if l < 4:
            value = jnp.where(row_real & (row_local == l), solved[...], value)
        acc[:, lanes] = value
        store(l).start()

    small.along_y()
    first.along_y()
    second.along_y()
    ycopy = candidates()
    small.along_z()
    first.along_z()
    small.arrive()
    tcopies = triangle()
    ycopies = share(ycopy)
    first.arrive()
    place(first, a1, b1)
    arrived(tcopies)
    payload()
    g.begin()
    c1.begin()
    second.along_z()
    g.step(1)
    c1.step(1)
    g.step(2)
    g.step(3)
    c1.step(2)
    g.step(4)
    second.arrive()
    place(second, a2, b2)
    g.step(5)
    c1.step(3)
    g.end()
    gcopy = push(gathered.at[core], gathered.at[core], across(dc=1))
    yrelays = relay(ycopies)
    c1.step(4)
    c2.begin()
    c1.step(5)
    arrived([gcopy] + yrelays)
    solve(0)
    c2.step(1)
    solve(1)
    solve(2)
    c2.step(2)
    solve(3)
    c1.end()
    c2.step(3)
    update(c1, 0, 0)
    c2.step(4)
    update(c1, 1, 1)
    c2.step(5)
    update(c1, 2, 2)
    c2.end()
    for l in range(3, BLK):
        update(c2, l - 3, l)
    for copy in sent:
        copy.wait_send()
    for l in range(BLK):
        store(l).wait()
    assert used[0] <= send.shape[0], used[0]


def run(step, panels, diag, rhs):
    cols = rhs.shape[0]
    anywhere = pl.BlockSpec(memory_space=pl.ANY)
    inside = pl.BlockSpec(memory_space=pltpu.VMEM)
    f32, bf16 = jnp.float32, jnp.bfloat16
    shapes = [
        (4, 2, 8, 8, NB), (4, 3, 8, 8, NB), (4, 3, 8, 8, NB),
        (8, 2, 8, NB), (8, 3, 8, NB), (8, 3, 8, NB),
        (8, 2, 8, NB), (8, 3, 8, NB), (8, 3, 8, NB),
        (4, 8, 3, 8, SPLIT), (8, 4, 3, 8, REST), (4, 8, 3, 8, SPLIT), (8, 4, 3, 8, REST),
        (2, 4, 8, 5, 8, NB),
        (2, 4, 8, 8, NB), (8, 4, 8, NB),
        (2, cols // 2, NB), (cols // 2, NB), (cols // 2, NB), (STEPS, 2, cols // 2, NB),
        (cols, NB),
    ]
    return pl.pallas_call(
        step_kernel,
        out_shape=jax.ShapeDtypeStruct(rhs.shape, f32),
        in_specs=[pl.BlockSpec(memory_space=pltpu.SMEM), inside, inside, anywhere],
        out_specs=anywhere,
        scratch_shapes=[pltpu.VMEM(shape, f32) for shape in shapes] + [
            pltpu.VMEM((cols, WIDE), bf16),
            pltpu.VMEM((cols, WIDE), bf16),
            pltpu.VMEM((NB, WIDE), bf16),
            pltpu.VMEM((NB, WIDE), bf16),
            pltpu.VMEM((cols, BLK * NB), f32),
            pltpu.SemaphoreType.DMA((224,)),
            pltpu.SemaphoreType.DMA((224,)),
            pltpu.SemaphoreType.DMA((16,)),
        ],
        compiler_params=pltpu.CompilerParams(
            collective_id=0, has_side_effects=True, vmem_limit_bytes=48 * 2**20),
        name="steps",
    )(step, panels, diag, rhs)


def body(step, rhs, panels, diag_inverses):
    parts = panels.reshape(BLK, 4, 8, 8, NB)
    inverse = diag_inverses.reshape(1, 4, 8, 8, NB)
    return run(step, parts, inverse, rhs.T).T


def solution(mesh):
    in_specs = (P(), P("row", "col"), P("row", "col"), P(None, "col"))
    out_specs = P("row", "col")
    return jax.shard_map(body, mesh=mesh, in_specs=in_specs, out_specs=out_specs, check_vma=False)
```

time: 551 us -> 113 us (0.21)
  waiting for transfers between devices: 455 us -> 0 us
  Pallas kernels: 0 us -> 104 us
  matrix products: 43.8 us -> 0 us
  local copies, waits for them, and re-layouts: 31.4 us -> 7.6 us
  between operations: 14.1 us -> 0.67 us
    psum x5 -> x0, waiting for transfers between devices: 455 us -> none  [broadcast(): return lax.psum(jnp.where(mine, value, jnp.zeros_like(value)), axis)]
    pallas_call x0 -> x1, Pallas kernels: none -> 104 us  [run(): pl.pallas_call(step_kernel, out_shape=jax.ShapeDtypeStruct(rhs.shape, f32...]
    dot_general x8 -> x0, matrix products: 43.8 us -> none  [the longest x4 34.3 us: apply_column(): jnp.einsum('bij,jk->bik', column, operand, precision=lax.Precision.HIGHEST)]
    reshape x2 -> x0, local copies, waits for them, and re-layouts: 12.1 us -> none  [the longest x1 6.13 us: body(): y_blocks = rhs.reshape(blk_local, width, cols_local)]
    select_n x1 -> x0, local copies, waits for them, and re-layouts: 6.06 us -> none  [body(): jnp.where((global_block == k)[:, None, None], solved[None], y_blocks)]
    unnamed x23 -> x5, local copies, waits for them, and re-layouts: 13.2 us -> 7.6 us
  transfers between devices with their start and end apart: 5 -> 0, of which waited for: 5 -> 0; matrix products, arithmetic and copies ran while one was open for 2% -> 0% of each run, Pallas kernels for 0% -> 0%
where the time goes in v1:
time: 113 us; the launch traced here: 112 us
  Pallas kernels  104 us (92%)
  local copies, waits for them, and re-layouts  7.6 us (7%)
    pallas_call x1, Pallas kernels, run(): pl.pallas_call(step_kernel, out_shape=jax.ShapeDtypeStruct(rhs.shape, f32...  104 us
    unnamed x5, local copies, waits for them, and re-layouts  7.6 us

profile of v1, /device:TPU:8, one launch (start us, length us, event | category | flops | bytes accessed | tf_op | source)
XLA Modules:
  0.0 111.9 jit_solution(1355483026059727893)
XLA Ops:
  0.7 0.0 copy-start
  0.7 1.4 %copy-done = f32[1536,256]{1,0:T(8,128)S(1)} copy-done((f32[1536,256]{1,0:T(8,128)S(1)}, f32[1536,256]{1,0:T(8,128)}, u32[]{:S(2)}) %copy-start) | copy-done | bytes 1572888
  2.1 0.0 copy-start.1
  2.1 0.9 copy-done.1
  3.0 103.6 %steps.1 = f32[864,1536]{1,0:T(8,128)} custom-call(s32[1]{0:T(128)S(6)} %copy.6.step, f32[6,4,8,8,256]{4,3,2,1,0:T(8,128)S(1)} %bitcast.4, f32[1,4,8,8,256]{4,3,2,1,0:T(8,128)S(1)} %bitcast.5, f32[864,1536]{1,0:T(8,128)} %bitcast.7), custom_call_target="tpu_custom_call" | custom-call | tf_op jit(solution)/shard_map/steps/pallas_call | solution.py:356
  106.6 5.2 %copy.7 = f32[1536,864]{0,1:T(8,128)} copy(f32[1536,864]{0,1:T(8,128)} %bitcast.6) | data formatting | bytes 10616832
Async XLA Ops:
  0.7 1.4 %copy-start = (f32[1536,256]{1,0:T(8,128)S(1)}, f32[1536,256]{1,0:T(8,128)}, u32[]{:S(2)}) copy-start(f32[1536,256]{1,0:T(8,128)} %param.6) | copy-start | bytes 4718596
  2.1 0.9 copy-start.1

commit v2 on v1

--- a/solution.py
+++ b/solution.py
@@ -45,8 +45,8 @@
     return result
 
 
-def step_kernel(step, panels, diag, rhs, out, r0, r1, r2, s0, s1, s2, p0, p1, p2, a1, b1, a2, b2, gathered,
-                tc, tall, ycand, ypart, yhalf, ysel, solved, high, low, f_high, f_low, acc, send, recv,
+def step_kernel(step, factor, diag, rhs, acc, panels, r0, r1, r2, s0, s1, s2, p0, p1, p2, a1, b1, a2, b2, gathered,
+                tc, tall, ycand, ypart, yhalf, ysel, solved, high, low, f_high, f_low, send, recv,
                 local):
     start = step[0]
     row, col = lax.axis_index("row"), lax.axis_index("col")
@@ -93,9 +93,12 @@
         pl.semaphore_signal(barrier, inc=1, device_id=friend, device_id_type=MESH)
     loads = [pltpu.make_async_copy(rhs.at[:, pl.ds(NB * l, NB)], acc.at[:, pl.ds(NB * l, NB)], local.at[l])
              for l in range(BLK)]
-    for load in loads:
+    fetches = [pltpu.make_async_copy(factor, panels, local.at[6]),
+               pltpu.make_async_copy(diag, tc.at[pl.ds(0, 1)], local.at[7])]
+    for load in fetches + loads:
         load.start()
-    tc[0] = diag[0]
+    for fetch in fetches:
+        fetch.wait()
     for ty in range(4):
         tc[1, ty] = choose(row_local, [panels[l, ty] for l in range(4)])
     pl.semaphore_wait(barrier, len(friends))
@@ -270,9 +273,6 @@
                     to = pl.ds(NB * i + source, n)
                     f_high[rows, to], f_low[rows, to] = halve(value)
 
-    def store(l):
-        return pltpu.make_async_copy(acc.at[:, pl.ds(NB * l, NB)], out.at[:, pl.ds(NB * l, NB)], local.at[8 + l])
-
     def update(chunk, p, l):
         assemble(chunk, p, l * 8 + row)
         lanes = pl.ds(NB * l, NB)
@@ -280,61 +280,59 @@
         if l < 4:
             value = jnp.where(row_real & (row_local == l), solved[...], value)
         acc[:, lanes] = value
-        store(l).start()
 
     small.along_y()
     first.along_y()
     second.along_y()
+    small.along_z()
     ycopy = candidates()
-    small.along_z()
-    first.along_z()
     small.arrive()
     tcopies = triangle()
+    first.along_z()
+    arrived(tcopies)
+    payload()
+    g.begin()
     ycopies = share(ycopy)
     first.arrive()
     place(first, a1, b1)
-    arrived(tcopies)
-    payload()
-    g.begin()
     c1.begin()
+    g.step(1)
     second.along_z()
-    g.step(1)
     c1.step(1)
     g.step(2)
+    second.arrive()
+    place(second, a2, b2)
+    c2.begin()
     g.step(3)
     c1.step(2)
+    c2.step(1)
     g.step(4)
-    second.arrive()
-    place(second, a2, b2)
+    c1.step(3)
     g.step(5)
-    c1.step(3)
+    c2.step(2)
     g.end()
     gcopy = push(gathered.at[core], gathered.at[core], across(dc=1))
+    c1.step(4)
     yrelays = relay(ycopies)
-    c1.step(4)
-    c2.begin()
+    c2.step(3)
     c1.step(5)
     arrived([gcopy] + yrelays)
     solve(0)
-    c2.step(1)
     solve(1)
+    c2.step(4)
     solve(2)
-    c2.step(2)
     solve(3)
+    c2.step(5)
     c1.end()
-    c2.step(3)
     update(c1, 0, 0)
-    c2.step(4)
     update(c1, 1, 1)
-    c2.step(5)
     update(c1, 2, 2)
     c2.end()
-    for l in range(3, BLK):
-        update(c2, l - 3, l)
+    update(c2,0,3)
+    update(c2,1,4)
+    update(c2,2,5)
     for copy in sent:
         copy.wait_send()
-    for l in range(BLK):
-        store(l).wait()
     assert used[0] <= send.shape[0], used[0]
 
 
@@ -344,6 +342,7 @@
     inside = pl.BlockSpec(memory_space=pltpu.VMEM)
     f32, bf16 = jnp.float32, jnp.bfloat16
     shapes = [
+        (BLK, 4, 8, 8, NB),
         (4, 2, 8, 8, NB), (4, 3, 8, 8, NB), (4, 3, 8, 8, NB),
         (8, 2, 8, NB), (8, 3, 8, NB), (8, 3, 8, NB),
         (8, 2, 8, NB), (8, 3, 8, NB), (8, 3, 8, NB),
@@ -355,15 +354,14 @@
     ]
     return pl.pallas_call(
         step_kernel,
-        out_shape=jax.ShapeDtypeStruct(rhs.shape, f32),
-        in_specs=[pl.BlockSpec(memory_space=pltpu.SMEM), inside, inside, anywhere],
-        out_specs=anywhere,
+        out_shape=pltpu.VMEM(rhs.shape, f32),
+        in_specs=[pl.BlockSpec(memory_space=pltpu.SMEM), anywhere, anywhere, anywhere],
+        out_specs=inside,
         scratch_shapes=[pltpu.VMEM(shape, f32) for shape in shapes] + [
             pltpu.VMEM((cols, WIDE), bf16),
             pltpu.VMEM((cols, WIDE), bf16),
             pltpu.VMEM((NB, WIDE), bf16),
             pltpu.VMEM((NB, WIDE), bf16),
-            pltpu.VMEM((cols, BLK * NB), f32),
             pltpu.SemaphoreType.DMA((224,)),
             pltpu.SemaphoreType.DMA((224,)),
             pltpu.SemaphoreType.DMA((16,)),

time: 113 us -> 99.1 us (0.88)
  Pallas kernels: 104 us -> 95 us
  local copies, waits for them, and re-layouts: 7.6 us -> 3.33 us
    pallas_call x1, Pallas kernels: 104 us -> 95 us  [run(): pl.pallas_call(step_kernel, out_shape=pltpu.VMEM(rhs.shape, f32), in_spec...]
    unnamed x5 -> x3, local copies, waits for them, and re-layouts: 7.6 us -> 3.33 us
where the time goes in v2:
time: 99.1 us; the launch traced here: 98.9 us
  Pallas kernels  95 us (96%)
  local copies, waits for them, and re-layouts  3.33 us (3%)
    pallas_call x1, Pallas kernels, run(): pl.pallas_call(step_kernel, out_shape=pltpu.VMEM(rhs.shape, f32), in_spec...  95 us
    unnamed x3, local copies, waits for them, and re-layouts  3.33 us

profile of v2, /device:TPU:8, one launch (start us, length us, event | category | flops | bytes accessed | tf_op | source)
XLA Modules:
  0.0 98.9 jit_solution(14170248799359922986)
XLA Ops:
  0.7 0.0 copy-start
  0.7 0.9 copy-done
  1.6 95.0 %steps.1 = f32[864,1536]{1,0:T(8,128)S(1)} custom-call(s32[1]{0:T(128)S(6)} %copy.7.step, f32[6,4,8,8,256]{4,3,2,1,0:T(8,128)} %bitcast.7, f32[1,4,8,8,256]{4,3,2,1,0:T(8,128)S(1)} %bitcast.5, f32[864,1536]{1,0:T(8,128)} %bitcast.6), custom_call_target="tpu_custom_call" | custom-call | tf_op jit(solution)/shard_map/steps/pallas_call | solution.py:355
  96.6 2.4 %copy.6 = f32[1536,864]{0,1:T(8,128)} copy(f32[1536,864]{0,1:T(8,128)S(1)} %bitcast.4) | data formatting | bytes 10616832
Async XLA Ops:
  0.7 1.0 copy-start

commit v3 on v2

--- a/solution.py
+++ b/solution.py
@@ -322,9 +322,9 @@
     c2.step(4)
     solve(2)
     solve(3)
-    c2.step(5)
     c1.end()
     update(c1, 0, 0)
+    c2.step(5)
     update(c1, 1, 1)
     update(c1, 2, 2)
     c2.end()

time: 99.1 us -> 99.3 us (level)
  no operation moved by 1% of the time
where the time goes in v3:
time: 99.3 us; the launch traced here: 99.2 us
  Pallas kernels  95.2 us (96%)
  local copies, waits for them, and re-layouts  3.33 us (3%)
    pallas_call x1, Pallas kernels, run(): pl.pallas_call(step_kernel, out_shape=pltpu.VMEM(rhs.shape, f32), in_spec...  95.2 us
    unnamed x3, local copies, waits for them, and re-layouts  3.33 us

profile of v3, /device:TPU:8, one launch (start us, length us, event | category | flops | bytes accessed | tf_op | source)
XLA Modules:
  0.0 99.2 jit_solution(9126832603468550457)
XLA Ops:
  0.7 0.0 copy-start
  0.7 0.9 copy-done
  1.6 95.2 %steps.1 = f32[864,1536]{1,0:T(8,128)S(1)} custom-call(s32[1]{0:T(128)S(6)} %copy.7.step, f32[6,4,8,8,256]{4,3,2,1,0:T(8,128)} %bitcast.7, f32[1,4,8,8,256]{4,3,2,1,0:T(8,128)S(1)} %bitcast.5, f32[864,1536]{1,0:T(8,128)} %bitcast.6), custom_call_target="tpu_custom_call" | custom-call | tf_op jit(solution)/shard_map/steps/pallas_call | solution.py:355
  96.8 2.4 %copy.6 = f32[1536,864]{0,1:T(8,128)} copy(f32[1536,864]{0,1:T(8,128)S(1)} %bitcast.4) | data formatting | bytes 10616832
Async XLA Ops:
  0.7 1.0 copy-start

commit v4 on v2

--- a/solution.py
+++ b/solution.py
@@ -187,15 +187,15 @@
             arrived(self.a_far)
 
     small = Scatter(tc, 0, 2, r0, s0, p0)
-    first = Scatter(panels, 0, 3, r1, s1, p1)
-    second = Scatter(panels, 3, 3, r2, s2, p2)
+    first = Scatter(panels, 0, 4, r1, s1, p1)
+    second = Scatter(panels, 4, 2, r2, s2, p2)
     g = Chunk(gathered.at[core], None, NB, 128)
     c1 = Chunk(a1, b1, SPLIT, 384)
     c2 = Chunk(a2, b2, SPLIT, 384)
 
     def place(scatter, a, b):
         for i in range(STEPS):
-            for p in range(3):
+            for p in range(scatter.n):
                 value = scatter.pick(i, p)
                 for in_a, lane, source, n in SEGMENTS[i]:
                     part = value[:, source:source + n]
@@ -327,10 +327,10 @@
     update(c1, 0, 0)
     update(c1, 1, 1)
     update(c1, 2, 2)
+    update(c1, 3, 3)
     c2.end()
-    update(c2,0,3)
-    update(c2,1,4)
-    update(c2,2,5)
+    update(c2, 0, 4)
+    update(c2, 1, 5)
     for copy in sent:
         copy.wait_send()
     assert used[0] <= send.shape[0], used[0]
@@ -343,10 +343,10 @@
     f32, bf16 = jnp.float32, jnp.bfloat16
     shapes = [
         (BLK, 4, 8, 8, NB),
-        (4, 2, 8, 8, NB), (4, 3, 8, 8, NB), (4, 3, 8, 8, NB),
-        (8, 2, 8, NB), (8, 3, 8, NB), (8, 3, 8, NB),
-        (8, 2, 8, NB), (8, 3, 8, NB), (8, 3, 8, NB),
-        (4, 8, 3, 8, SPLIT), (8, 4, 3, 8, REST), (4, 8, 3, 8, SPLIT), (8, 4, 3, 8, REST),
+        (4, 2, 8, 8, NB), (4, 4, 8, 8, NB), (4, 2, 8, 8, NB),
+        (8, 2, 8, NB), (8, 4, 8, NB), (8, 2, 8, NB),
+        (8, 2, 8, NB), (8, 4, 8, NB), (8, 2, 8, NB),
+        (4, 8, 4, 8, SPLIT), (8, 4, 4, 8, REST), (4, 8, 2, 8, SPLIT), (8, 4, 2, 8, REST),
         (2, 4, 8, 5, 8, NB),
         (2, 4, 8, 8, NB), (8, 4, 8, NB),
         (2, cols // 2, NB), (cols // 2, NB), (cols // 2, NB), (STEPS, 2, cols // 2, NB),

time: 99.1 us -> 102 us (1.029)
  the two profiles are of different devices: /device:TPU:8 before, /device:TPU:1 now
where the time goes in v4:
time: 102 us
  Pallas kernels  97.8 us (96%)
  local copies, waits for them, and re-layouts  3.33 us (3%)
    pallas_call x1, Pallas kernels, run(): pl.pallas_call(step_kernel, out_shape=pltpu.VMEM(rhs.shape, f32), in_spec...  97.8 us
    unnamed x3, local copies, waits for them, and re-layouts  3.33 us

profile of v4, /device:TPU:1, one launch (start us, length us, event | category | flops | bytes accessed | tf_op | source)
XLA Modules:
  0.0 101.8 jit_solution(11027586787948686368)
XLA Ops:
  0.7 0.0 copy-start
  0.7 0.9 copy-done
  1.6 97.8 %steps.1 = f32[864,1536]{1,0:T(8,128)S(1)} custom-call(s32[1]{0:T(128)S(6)} %copy.7.step, f32[6,4,8,8,256]{4,3,2,1,0:T(8,128)} %bitcast.7, f32[1,4,8,8,256]{4,3,2,1,0:T(8,128)S(1)} %bitcast.5, f32[864,1536]{1,0:T(8,128)} %bitcast.6), custom_call_target="tpu_custom_call" | custom-call | tf_op jit(solution)/shard_map/steps/pallas_call | solution.py:355
  99.4 2.4 %copy.6 = f32[1536,864]{0,1:T(8,128)} copy(f32[1536,864]{0,1:T(8,128)S(1)} %bitcast.4) | data formatting | bytes 10616832
Async XLA Ops:
  0.7 1.0 copy-start
